TPU v7x, 32 devices: a whole 2x2x4 slice. The times are simulated.
32 devices in a mesh: dp: 8 (over y, x, core), tensor: 4 (over z).
Axes of the slice: x: 2, y: 2, z: 4, core: 2. Of those that a mesh axis runs over, the one named last changes fastest.
Arguments:
- tokens: bfloat16 [16384, 2048], P('dp'), may hold values from -6 to 6
- segments: int32 [16384], P('dp'), may hold values from 0 to 10, as said below
- positions: int32 [16384], P('dp'), may hold values from 0 to 4046, as said below
- ln1_gain: float32 [2048], replicated, may hold values from 0.25 to 1.75
- ln1_bias: float32 [2048], replicated, may hold values from -2 to 2
- ln2_gain: float32 [2048], replicated, may hold values from 0.25 to 1.75
- ln2_bias: float32 [2048], replicated, may hold values from -2 to 2
- qkv_weight: bfloat16 [2048, 6144], P(None, 'tensor'), may hold values from -0.125 to 0.125
- dense_weight: bfloat16 [2048, 2048], P('tensor'), may hold values from -1 to 1
- fc1_weight: bfloat16 [2048, 8192], P(None, 'tensor'), may hold values from -0.125 to 0.125
- fc2_weight: bfloat16 [8192, 2048], P('tensor'), may hold values from -0.0625 to 0.0625
- upstream: bfloat16 [16384, 2048], P('dp', 'tensor'), may hold values from -6 to 6
Outputs:
- output: bfloat16 [16384, 2048], P('dp', 'tensor')
- input_grad: float32 [16384, 2048], P('dp')
- qkv_grad: float32 [2048, 6144], P('dp', 'tensor')
- dense_grad: float32 [2048, 2048], P('tensor', 'dp')
- fc1_grad: float32 [2048, 8192], P('dp', 'tensor')
- fc2_grad: float32 [8192, 2048], P('tensor', 'dp')
- ln1_gain_grad: float32 [2048], P('dp')
- ln1_bias_grad: float32 [2048], P('dp')
- ln2_gain_grad: float32 [2048], P('dp')
- ln2_bias_grad: float32 [2048], P('dp')
Inputs may be any that keep to these rules, and one draw needn't show every extreme that they name: `segments`: within each sequence of 2048 tokens the numbers start at 0 and rise by one at each document's start; a document holds 200 to 2000 tokens, the last one of a sequence may be cut shorter. `positions`: A token's place in its document plus an offset below 2048 drawn for that document.
All inputs are finite; a program needn't handle non-finite values.
Results may differ from a plain program's by a relative error of at most 0.012.
Values may be sent and summed in bfloat16 or wider, within the bound.
A program may use at most 384 MiB of HBM per device.

v0:
```python
import functools
import itertools

import jax
import jax.numpy as jnp
from jax import lax
from jax.experimental import pallas as pl
from jax.experimental.pallas import tpu as pltpu
from jax.sharding import PartitionSpec as P

HEAD_DIM = 256
ROT_DIM = 64
SEQ_LEN = 2048
LANES = 128
VMEM_CAP = 60 * 2**20
NT = (((1,), (1,)), ((), ()))
TN = (((0,), (0,)), ((), ()))


def rot_tables(positions):
    half = ROT_DIM // 2
    steps_up = jnp.arange(half).astype(jnp.float32) * 2.0 / ROT_DIM
    inverse = jnp.power(jnp.float32(10000.0), -steps_up)
    angle = inverse[:, None] * positions.astype(jnp.float32)[None, :]
    return jnp.concatenate([jnp.cos(angle), jnp.sin(angle)], 0)


def rot_tiles(table):
    half = ROT_DIM // 2
    cos, sin = table[:half], table[half:]
    zero = jnp.zeros_like(sin)
    rest = jnp.zeros((LANES - ROT_DIM, table.shape[1]), jnp.float32)
    rows = ((cos, cos, rest + 1.0), (-sin, zero, rest), (zero, sin, rest))
    return tuple(jnp.concatenate(parts, 0).T for parts in rows)


def rotate_tile(u, cos_t, sin_up, sin_down):
    half = ROT_DIM // 2
    return u * cos_t + pltpu.roll(u, LANES - half, 1) * sin_up + pltpu.roll(u, half, 1) * sin_down


def rotate_back_tile(g, cos_t, sin_up, sin_down):
    half = ROT_DIM // 2
    return g * cos_t + pltpu.roll(g * sin_down, LANES - half, 1) + pltpu.roll(g * sin_up, half, 1)


def pre_kernel(x_ref, g1_ref, b1_ref, g2_ref, b2_ref, rot_ref, w_ref, h1_ref, h2_ref, qkv_ref, stats_ref):
    x = x_ref[...].astype(jnp.float32)
    mean = jnp.mean(x, axis=-1, keepdims=True)
    center = x - mean
    inv = lax.rsqrt(jnp.mean(center * center, axis=-1, keepdims=True) + 1e-05)
    stats_ref[:, :1] = mean
    stats_ref[:, 1:] = inv
    normed = center * inv
    h1 = (normed * g1_ref[...] + b1_ref[...]).astype(jnp.bfloat16)
    h1_ref[...] = h1
    h2_ref[...] = (normed * g2_ref[...] + b2_ref[...]).astype(jnp.bfloat16)
    cos_t, su, sd = rot_tiles(rot_ref[...])
    for b in range(w_ref.shape[1] // HEAD_DIM):
        cols = slice(b * HEAD_DIM, (b + 1) * HEAD_DIM)
        y = jnp.dot(h1, w_ref[:, cols], preferred_element_type=jnp.float32)
        if b % 3 < 2:
            qkv_ref[:, b * HEAD_DIM : b * HEAD_DIM + LANES] = rotate_tile(y[:, :LANES], cos_t, su, sd).astype(jnp.bfloat16)
            qkv_ref[:, b * HEAD_DIM + LANES : (b + 1) * HEAD_DIM] = y[:, LANES:].astype(jnp.bfloat16)
        else:
            qkv_ref[:, cols] = y.astype(jnp.bfloat16)


def project(tokens, g1, b1, g2, b2, rot, w, rows=512):
    total, width = tokens.shape
    rows = min(rows, total)
    row_blk = lambda cols: pl.BlockSpec((rows, cols), lambda i: (i, 0))
    vec = pl.BlockSpec((1, width), lambda i: (0, 0))
    cols = w.shape[1]
    return pl.pallas_call(
        pre_kernel,
        grid=(total // rows,),
        in_specs=[row_blk(width), vec, vec, vec, vec, pl.BlockSpec((ROT_DIM, rows), lambda i: (0, i)),
                  pl.BlockSpec((width, cols), lambda i: (0, 0), pipeline_mode=pl.Buffered(1))],
        out_specs=[row_blk(width), row_blk(width), row_blk(cols), row_blk(2)],
        out_shape=[jax.ShapeDtypeStruct((total, width), jnp.bfloat16)] * 2 + [jax.ShapeDtypeStruct((total, cols), jnp.bfloat16), jax.ShapeDtypeStruct((total, 2), jnp.float32)],
        compiler_params=pltpu.CompilerParams(vmem_limit_bytes=VMEM_CAP),
        cost_estimate=pl.CostEstimate(flops=2 * total * width * cols, bytes_accessed=6 * total * width + 2 * cols * (width + total), transcendentals=0),
        name="norm_project",
    )(tokens, g1[None], b1[None], g2[None], b2[None], rot, w)


def attend_kernel(block, heads, qkv_ref, drow_ref, dcol_ref, o_ref, lse_ref, v_turned):
    i = pl.program_id(1)
    scale = HEAD_DIM ** (-0.5)
    part = lambda h, c: slice((3 * h + c) * HEAD_DIM, (3 * h + c + 1) * HEAD_DIM)

    @pl.when(i == 0)
    def _():
        for h in range(heads):
            v_turned[h] = qkv_ref[:, part(h, 2)].T

    here = pl.ds(pl.multiple_of(i * block, block), block)
    queries = [qkv_ref[here, part(h, 0)] * jnp.bfloat16(scale) for h in range(heads)]
    docs_q = drow_ref[...]
    later = lax.broadcasted_iota(jnp.int32, (block, block), 1) >= lax.broadcasted_iota(jnp.int32, (block, block), 0)

    def body(j, carry, corner=False):
        rows = pl.ds(pl.multiple_of(j * block, block), block)
        allowed = docs_q == dcol_ref[rows, :]
        if corner:
            allowed = allowed & later
        new = []
        for h in range(heads):
            m, l, acc = carry[h]
            s = lax.dot_general(qkv_ref[rows, part(h, 1)], queries[h], NT, preferred_element_type=jnp.float32)
            s = jnp.where(allowed, s, -1e30)
            m_new = jnp.maximum(m, jnp.max(s, axis=0, keepdims=True))
            p = jnp.exp(s - m_new)
            alpha = jnp.exp(m - m_new)
            l = l * alpha + jnp.sum(p, axis=0, keepdims=True)
            acc = acc * alpha + jnp.dot(v_turned[h, :, rows], p.astype(jnp.bfloat16), preferred_element_type=jnp.float32)
            new.append((m_new, l, acc))
        return tuple(new)

    start = (jnp.full((1, block), -1e30, jnp.float32), jnp.zeros((1, block), jnp.float32), jnp.zeros((HEAD_DIM, block), jnp.float32))
    carry = body(i, lax.fori_loop(0, i, body, (start,) * heads), True)
    for h in range(heads):
        m, l, acc = carry[h]
        o_ref[:, h * HEAD_DIM : (h + 1) * HEAD_DIM] = (acc * (1.0 / l)).T.astype(jnp.bfloat16)
        lse_ref[h] = m + jnp.log(l)


def attend(qkv, docs, block=512):
    total, cols = qkv.shape
    heads = cols // (3 * HEAD_DIM)
    seqs = total // SEQ_LEN
    n = SEQ_LEN // block
    return pl.pallas_call(
        functools.partial(attend_kernel, block, heads),
        grid=(seqs, n),
        in_specs=[
            pl.BlockSpec((SEQ_LEN, cols), lambda s, i: (s, 0)),
            pl.BlockSpec((1, block), lambda s, i: (0, s * n + i)),
            pl.BlockSpec((SEQ_LEN, 1), lambda s, i: (s, 0)),
        ],
        out_specs=[pl.BlockSpec((block, heads * HEAD_DIM), lambda s, i: (s * n + i, 0)),
                   pl.BlockSpec((heads, 1, block), lambda s, i: (0, 0, s * n + i))],
        out_shape=[jax.ShapeDtypeStruct((total, heads * HEAD_DIM), jnp.bfloat16), jax.ShapeDtypeStruct((heads, 1, total), jnp.float32)],
        scratch_shapes=[pltpu.VMEM((heads, HEAD_DIM, SEQ_LEN), jnp.bfloat16)],
        compiler_params=pltpu.CompilerParams(vmem_limit_bytes=VMEM_CAP),
        cost_estimate=pl.CostEstimate(flops=2 * total * SEQ_LEN * heads * HEAD_DIM, bytes_accessed=4 * total * cols, transcendentals=total * SEQ_LEN),
        name="attend",
    )(qkv, docs[None, :], docs[:, None])


def finish_kernel(x_ref, stats_ref, s_ref, up_ref, out_ref):
    mean, inv = stats_ref[:, :1], stats_ref[:, 1:]
    s = s_ref[...].astype(jnp.float32)
    center = x_ref[...].astype(jnp.float32) - mean
    bend = jnp.mean(s * center, axis=-1, keepdims=True) * (inv * inv * inv)
    level = jnp.mean(s, axis=-1, keepdims=True) * inv
    out_ref[...] = (up_ref[...].astype(jnp.float32) - level) + (s * inv - center * bend)


def finish(tokens, stats, s, up, rows=512):
    total, width = tokens.shape
    block = pl.BlockSpec((min(rows, total), width), lambda i: (i, 0))
    return pl.pallas_call(
        finish_kernel,
        grid=(total // min(rows, total),),
        in_specs=[block, pl.BlockSpec((min(rows, total), 2), lambda i: (i, 0)), block, block],
        out_specs=block,
        out_shape=jax.ShapeDtypeStruct((total, width), jnp.float32),
        compiler_params=pltpu.CompilerParams(vmem_limit_bytes=VMEM_CAP),
        cost_estimate=pl.CostEstimate(flops=10 * total * width, bytes_accessed=10 * total * width, transcendentals=0),
        name="finish",
    )(tokens, stats, s, up)


AX = "tensor"
DP = "dp"
MESH = pl.DeviceIdType.MESH
STRIP = 256


def greet(peers):
    barrier = pltpu.get_barrier_semaphore()
    count = 0
    for cond, device in peers:
        @pl.when(cond)
        def _(device=device):
            pl.semaphore_signal(barrier, inc=1, device_id=device, device_id_type=MESH)
        count = count + jnp.asarray(cond).astype(jnp.int32)
    pl.semaphore_wait(barrier, count)


def within(c, count):
    return (c >= 0) & (c < count)


def blend(first, second):
    both = [(place / len(one), which, entry) for which, one in enumerate((first, second)) for place, entry in enumerate(one)]
    return [entry for _, _, entry in sorted(both, key=lambda e: e[:2])]


class LineSum:
    def __init__(self, n, chunks, full_ref, own, recv, rs_send, rs_recv, ag_right, ag_left, ag_recv, store_sem):
        self.n, self.chunks, self.full_ref, self.own, self.recv = n, chunks, full_ref, own, recv
        self.rs_send, self.rs_recv, self.ag_send, self.ag_recv, self.store_sem = rs_send, rs_recv, (ag_right, ag_left), ag_recv, store_sem
        self.k = lax.axis_index(AX)
        self.rows, self.cols = own.shape[2], own.shape[3]

    def block(self, c, j):
        return self.full_ref.at[pl.ds(pl.multiple_of(c * self.rows, self.rows), self.rows), pl.ds(j * self.cols, self.cols)]

    def copy(self, src, dst, send, recv, right):
        return pltpu.make_async_remote_copy(src, dst, send, recv, device_id={AX: self.k + 1 if right else self.k - 1}, device_id_type=MESH)

    def scatter_copy(self, c, j, right):
        slot = j if right else jnp.where(self.k - 1 == j, self.n, j)
        return self.copy(self.own.at[c, j], self.recv.at[c, slot], self.rs_send.at[c, j], self.rs_recv.at[c, slot], right)

    def scatter_arrived(self, c, slot):
        dst = self.recv.at[c, slot]
        pltpu.make_async_copy(dst, dst, self.rs_recv.at[c, slot]).wait()

    def gather_copy(self, c, j, right, src=None):
        block = self.block(c, j)
        return self.copy(block if src is None else src, block, self.ag_send[0 if right else 1].at[c, j], self.ag_recv.at[c, j], right)

    def gather_arrived(self, c, j):
        block = self.block(c, j)
        pltpu.make_async_copy(block, block, self.ag_recv.at[c, j]).wait()

    def store(self, c, j):
        return pltpu.make_async_copy(self.own.at[c, j], self.block(c, j), self.store_sem.at[c])

    def pieces(self, i):
        return [functools.partial(self.pass_on, i, p) for p in range(self.n)] + [functools.partial(self.close, i)]

    def pass_on(self, i, p):
        n, k, chunks = self.n, self.k, self.chunks
        for right in (True, False):
            j = p if right else n - 1 - p
            dist = (k - j) if right else (j - k)
            onward = (k < n - 1) if right else (k > 0)
            behind = (k > 0) if right else (k < n - 1)
            c_gather = i - (n - 1) - dist
            c_scatter = i - (k if right else n - 1 - k)

            @pl.when((dist > 0) & within(c_gather, chunks))
            def _(j=j, right=right, c=c_gather, onward=onward):
                self.gather_arrived(c, j)

                @pl.when(onward)
                def _():
                    self.gather_copy(c, j, right).start()

            @pl.when((dist < 0) & within(c_scatter, chunks))
            def _(j=j, right=right, c=c_scatter, behind=behind):
                @pl.when(behind)
                def _():
                    self.scatter_arrived(c, j)
                    self.own[c, j] = self.own[c, j] + self.recv[c, j]

                self.scatter_copy(c, j, right).start()

    def close(self, i):
        n, k, chunks = self.n, self.k, self.chunks
        c = i - (n - 1)
        for j in range(n):
            @pl.when((k == j) & within(c, chunks))
            def _(j=j):
                total = self.own[c, j].astype(jnp.float32)
                if j > 0:
                    self.scatter_arrived(c, j)
                    total = total + self.recv[c, j].astype(jnp.float32)
                if j < n - 1:
                    self.scatter_arrived(c, n)
                    total = total + self.recv[c, n].astype(jnp.float32)
                self.own[c, j] = total.astype(self.own.dtype)
                self.store(c, j).start()
                if j < n - 1:
                    self.gather_copy(c, j, True, self.own.at[c, j]).start()
                if j > 0:
                    self.gather_copy(c, j, False, self.own.at[c, j]).start()

    def drain(self):
        n, k = self.n, self.k

        def one(c, _):
            for j in range(n):
                @pl.when(k < j)
                def _(j=j):
                    self.scatter_copy(c, j, True).wait_send()

                    @pl.when(k > 0)
                    def _():
                        self.gather_copy(c, j, False).wait_send()

                @pl.when(k > j)
                def _(j=j):
                    self.scatter_copy(c, j, False).wait_send()

                    @pl.when(k < n - 1)
                    def _():
                        self.gather_copy(c, j, True).wait_send()

                @pl.when(k == j)
                def _(j=j):
                    self.store(c, j).wait()
                    if j < n - 1:
                        self.gather_copy(c, j, True, self.own.at[c, j]).wait_send()
                    if j > 0:
                        self.gather_copy(c, j, False, self.own.at[c, j]).wait_send()
            return 0

        lax.fori_loop(0, self.chunks, one, 0)


class HalvingSum:
    def __init__(self, dp, groups, xs, ys, outs, xbuf, ybuf, tiles, recvs, stage, stage_turned, x_sem, y_sem, send_sem, recv_sem, out_sem):
        self.dp, self.bits = dp, dp.bit_length() - 1
        self.groups, self.xs, self.ys, self.outs = groups, xs, ys, outs
        self.xbuf, self.ybuf, self.tiles, self.recvs = xbuf, ybuf, tiles, recvs
        self.stage, self.stage_turned = stage, stage_turned
        self.x_sem, self.y_sem, self.send_sem, self.recv_sem, self.out_sem = x_sem, y_sem, send_sem, recv_sem, out_sem
        self.me = lax.axis_index(DP)
        self.slots = tiles.shape[0]
        self.width = tiles.shape[-1]
        self.first = [sum(g["count"] for g in groups[:i]) for i in range(len(groups) + 1)]
        self.total = self.first[-1]
        self.lags = [1] + [1 + 2 * level for level in range(1, self.bits - 1)] + [max(2 * self.bits - 2, 2)]

    def bit(self, b):
        return lax.rem(lax.div(self.me, 2**b), 2)

    def partner(self, b):
        return self.me + (1 - 2 * self.bit(b)) * 2**b

    def order(self, odd):
        rest = list(range(1, self.bits))
        return [0] + (rest[1:] + rest[:1] if odd else rest)

    def pick(self, odd, level, value):
        done = self.order(odd)[:level]
        now = self.order(odd)[level]
        return tuple(0 if b in done else value if b == now else slice(None) for b in range(self.bits))

    def in_group(self, t, g):
        return (t >= self.first[g]) & (t < self.first[g + 1])

    def x_copies(self, t):
        for g, group in enumerate(self.groups):
            at = pl.ds(pl.multiple_of((t - self.first[g]) * STRIP, STRIP), STRIP)
            slot = lax.rem(t, 2)
            yield self.in_group(t, g), pltpu.make_async_copy(self.xs[group["x"]].at[:, at], self.xbuf.at[slot], self.x_sem.at[slot])

    def x_start(self, t):
        for cond, copy in self.x_copies(t):
            @pl.when(cond)
            def _(copy=copy):
                copy.start()

    def x_wait(self, t):
        slot = lax.rem(t, 2)
        pltpu.make_async_copy(self.xbuf.at[slot], self.xbuf.at[slot], self.x_sem.at[slot]).wait()

    def y_copy(self, g):
        y = self.groups[g]["y"]
        return pltpu.make_async_copy(self.ys[y], self.ybuf.at[y % 2], self.y_sem.at[y % 2])

    def send(self, u, odd, level):
        slot = lax.rem(u, self.slots)
        return pltpu.make_async_remote_copy(
            self.tiles.at[(slot, *self.pick(odd, level, 1))], self.recvs[level].at[slot],
            self.send_sem.at[level, slot], self.recv_sem.at[level, slot],
            device_id={DP: self.partner(self.order(odd)[level])}, device_id_type=MESH)

    def out_copies(self, u):
        slot = lax.rem(u, 2)
        for g, group in enumerate(self.groups):
            at = pl.ds(pl.multiple_of((u - self.first[g]) * STRIP, STRIP), STRIP)
            out = self.outs[group["out"]]
            if group["turned"]:
                yield self.in_group(u, g), pltpu.make_async_copy(self.stage_turned.at[slot], out.at[:, at], self.out_sem.at[slot])
            else:
                yield self.in_group(u, g), pltpu.make_async_copy(self.stage.at[slot], out.at[at, :], self.out_sem.at[slot])

    def out_wait(self, u):
        for cond, copy in self.out_copies(u):
            @pl.when(cond)
            def _(copy=copy):
                copy.wait()

    def prologue(self):
        self.x_start(jnp.int32(0))
        self.y_copy(0).start()
        for g in range(1, len(self.groups)):
            if self.groups[g]["y"] == 1:
                self.y_copy(g).start()
                break

    def pieces(self, t, place, period, parts=4):
        odd = place % 2
        share = max(self.dp // parts, 1)
        spans = [range(first, first + share) for first in range(0, self.dp, share)]
        return [functools.partial(self.halve, t, place, period)] + [
            functools.partial(self.multiply, t, place, period, span, span[0] == 0, span[-1] == self.dp - 1) for span in spans]

    def halve(self, t, place, period):
        for level in range(self.bits - 1, -1, -1):
            u = t - self.lags[level]
            u_odd = (place - self.lags[level]) % period % 2

            @pl.when(within(u, self.total))
            def _(u=u, u_odd=u_odd, level=level):
                slot = lax.rem(u, self.slots)
                got = self.recvs[level]
                pltpu.make_async_copy(got.at[slot], got.at[slot], self.recv_sem.at[level, slot]).wait()
                keep = (slot, *self.pick(u_odd, level, 0))
                if level < self.bits - 1:
                    left = [range(2) if isinstance(p, slice) else (p,) for p in keep[1:]]
                    for flat, idx in enumerate(itertools.product(*left)):
                        pos = tuple(int(b) for b in format(flat, "b").zfill(self.bits - 1 - level))
                        self.tiles[(slot, *idx)] = self.tiles[(slot, *idx)] + got[(slot, *pos)]
                    self.send(u, u_odd, level + 1).start()
                else:
                    @pl.when(u >= 2)
                    def _():
                        self.out_wait(u - 2)

                    value = self.tiles[keep].astype(jnp.float32) + got[slot].astype(jnp.float32)
                    for g, group in enumerate(self.groups):
                        @pl.when(self.in_group(u, g))
                        def _(group=group):
                            if group["turned"]:
                                self.stage_turned[lax.rem(u, 2)] = value.T
                            else:
                                self.stage[lax.rem(u, 2)] = value
                    for cond, copy in self.out_copies(u):
                        @pl.when(cond)
                        def _(copy=copy):
                            copy.start()

    def ready(self, t, place, period):
        @pl.when(t >= self.slots)
        def _():
            for level in range(self.bits):
                self.send(t - self.slots, (place - self.slots) % period % 2, level).wait_send()

        seen = []
        for g, group in enumerate(self.groups):
            if group["y"] in seen:
                continue
            seen.append(group["y"])

            @pl.when(t == self.first[g])
            def _(g=g, group=group):
                self.y_copy(g).wait()
                if group["y"] == 1:
                    for later in range(len(self.groups)):
                        if self.groups[later]["y"] == 2:
                            self.y_copy(later).start()
                            break

        @pl.when(t + 1 < self.total)
        def _():
            self.x_start(t + 1)

        self.x_wait(t)

    def multiply(self, t, place, period, span, opens, closes):
        @pl.when(within(t, self.total))
        def _():
            if opens:
                self.ready(t, place, period)
            slot = lax.rem(t, self.slots)
            y_slot = jnp.int32(0)
            for g, group in enumerate(self.groups):
                y_slot = jnp.where(t >= self.first[g], group["y"] % 2, y_slot)
            x = self.xbuf[lax.rem(t, 2)]
            for flat in span:
                idx = tuple((flat >> b) & 1 for b in range(self.bits))
                shard = sum((self.bit(b) + idx[b] * (1 - 2 * self.bit(b))) * 2**b for b in range(self.bits))
                at = pl.ds(pl.multiple_of(shard * self.width, self.width), self.width)
                self.tiles[(slot, *idx)] = lax.dot_general(x, self.ybuf[y_slot, :, at], TN, preferred_element_type=jnp.float32).astype(jnp.bfloat16)
            if closes:
                self.send(t, place % 2, 0).start()

    def drain(self, period):
        for u in range(self.total - self.slots, self.total):
            for level in range(self.bits):
                self.send(jnp.int32(u), u % period % 2, level).wait_send()
        for u in range(self.total - 2, self.total):
            self.out_wait(jnp.int32(u))


class LineScatter:
    def __init__(self, n, own, recv, x_own, out_ref, send_sem, recv_sem, store_sem, hop=1):
        self.hop = hop
        self.n, self.own, self.recv, self.x_own, self.out_ref = n, own, recv, x_own, out_ref
        self.send_sem, self.recv_sem, self.store_sem = send_sem, recv_sem, store_sem
        self.k = lax.axis_index(AX)
        self.chunks, _, self.rows, self.cols = own.shape

    def span(self, c):
        return pl.ds(pl.multiple_of(c * self.rows, self.rows), self.rows)

    def copy(self, c, j, right):
        slot = j if right else jnp.where(self.k - 1 == j, self.n, j)
        return pltpu.make_async_remote_copy(
            self.own.at[c, j], self.recv.at[c, slot], self.send_sem.at[c, j], self.recv_sem.at[c, slot],
            device_id={AX: self.k + 1 if right else self.k - 1}, device_id_type=MESH)

    def arrived(self, c, slot):
        got = self.recv.at[c, slot]
        pltpu.make_async_copy(got, got, self.recv_sem.at[c, slot]).wait()

    def store(self, c, j):
        return pltpu.make_async_copy(self.own.at[c, j], self.out_ref.at[self.span(c), :], self.store_sem.at[c])

    def pieces(self, i):
        return [functools.partial(self.pass_on, i, p) for p in range(self.n)] + [functools.partial(self.close, i)]

    def step(self, i):
        for piece in self.pieces(i):
            piece()

    def pass_on(self, i, p):
        n, k = self.n, self.k
        for right in (True, False):
            j = p if right else n - 1 - p
            ahead = (j > k) if right else (j < k)
            behind = (k > 0) if right else (k < n - 1)
            c = i - self.hop * (k if right else n - 1 - k)

            @pl.when(ahead & within(c, self.chunks))
            def _(j=j, right=right, c=c, behind=behind):
                @pl.when(behind)
                def _():
                    self.arrived(c, j)
                    self.own[c, j] = self.own[c, j] + self.recv[c, j]

                self.copy(c, j, right).start()

    def close(self, i):
        n, k = self.n, self.k
        c = i - self.hop * (n - 1)
        for j in range(n):
            @pl.when((k == j) & within(c, self.chunks))
            def _(j=j):
                total = self.x_own[self.span(c), :].astype(jnp.float32) + self.own[c, j].astype(jnp.float32)
                if j > 0:
                    self.arrived(c, j)
                    total = total + self.recv[c, j].astype(jnp.float32)
                if j < n - 1:
                    self.arrived(c, n)
                    total = total + self.recv[c, n].astype(jnp.float32)
                self.own[c, j] = total.astype(self.own.dtype)
                self.store(c, j).start()

    def drain(self):
        def one(c, _):
            for j in range(self.n):
                @pl.when(self.k < j)
                def _(j=j):
                    self.copy(c, j, True).wait_send()

                @pl.when(self.k > j)
                def _(j=j):
                    self.copy(c, j, False).wait_send()

                @pl.when(self.k == j)
                def _(j=j):
                    self.store(c, j).wait()
            return 0

        lax.fori_loop(0, self.chunks, one, 0)


def scatter_scratch(n, chunks, rows, cols):
    low, dma = jnp.bfloat16, pltpu.SemaphoreType.DMA
    return [pltpu.VMEM((chunks, n, rows, cols), low), pltpu.VMEM((chunks, n + 1, rows, cols), low), pltpu.VMEM((chunks * rows, cols), low),
            dma((chunks, n)), dma((chunks, n + 1)), dma((chunks,))]


class Stream:
    def __init__(self, hbm, slots, sem, inward):
        self.hbm, self.slots, self.sem, self.inward = hbm, slots, sem, inward
        self.rows = slots.shape[1]

    def copy(self, p):
        at = self.hbm.at[pl.ds(pl.multiple_of(p * self.rows, self.rows), self.rows), :]
        slot = lax.rem(p, 2)
        pair = (at, self.slots.at[slot]) if self.inward else (self.slots.at[slot], at)
        return pltpu.make_async_copy(*pair, self.sem.at[slot])


class Terms:
    def __init__(self, n, own, sums, w, gains, streams):
        self.n, self.own, self.sums, self.w, self.gains, self.streams = n, own, sums, w, gains, streams
        self.rows, self.cols = streams[0].rows, own.shape[3]
        self.blocks = own.shape[0] * own.shape[2] // self.rows

    def start(self, i):
        for stream in self.streams:
            stream.copy(i).start()

    def pieces(self, i):
        return [functools.partial(self.tile, i, j) for j in range(self.n)]

    def tile(self, i, j):
        @pl.when(i < self.blocks)
        def _():
            if j == 0:
                @pl.when(i + 1 < self.blocks)
                def _():
                    self.start(i + 1)

                for stream in self.streams:
                    stream.copy(i).wait()
            two = lax.rem(i, 2)
            x, stats, gq, gh2 = (stream.slots for stream in self.streams)
            at = slice(j * self.cols, (j + 1) * self.cols)
            mean, inv = stats[two, :, :1], stats[two, :, 1:]
            one = lax.dot_general(gq[two], self.w[at, :], NT, preferred_element_type=jnp.float32)
            other = gh2[two, :, at].astype(jnp.float32)
            normed = (x[two, :, at].astype(jnp.float32) - mean) * inv
            total = (one * self.gains[:1, at] + other * self.gains[1:, at]).astype(self.own.dtype)
            height = self.own.shape[2]
            for b in range(self.rows // height):
                self.own[i * (self.rows // height) + b, j] = total[b * height : (b + 1) * height]
            for row, value in enumerate((one * normed, one, other * normed, other)):
                self.sums[row : row + 1, at] += jnp.sum(value, axis=0, keepdims=True)


class SmallSum:
    def __init__(self, n, bits, partner, out_ref, acc, dp_recv, line_send, line_recv, sems):
        self.n, self.bits, self.partner = n, bits, partner
        self.out_ref, self.acc, self.dp_recv, self.line_send, self.line_recv = out_ref, acc, dp_recv, line_send, line_recv
        self.dp_send_sem, self.dp_recv_sem, self.line_send_sem, self.line_recv_sem, self.own_sem = sems
        self.k, self.me = lax.axis_index(AX), lax.axis_index(DP)

    def last(self):
        return pltpu.make_async_copy(self.dp_recv.at[0, :, pl.ds(0, self.out_ref.shape[1])], self.out_ref, self.own_sem.at[0])

    def swap(self, b):
        return pltpu.make_async_remote_copy(
            self.acc, self.dp_recv.at[b], self.dp_send_sem.at[b], self.dp_recv_sem.at[b], device_id={DP: self.partner(b)}, device_id_type=MESH)

    def onward(self, way):
        return pltpu.make_async_remote_copy(
            self.line_send.at[way], self.line_recv.at[way], self.line_send_sem.at[way], self.line_recv_sem.at[way],
            device_id={AX: self.k + 1 - 2 * way}, device_id_type=MESH)

    def step(self, i):
        n, k = self.n, self.k
        for b in range(self.bits + 1):
            @pl.when(i == b)
            def _(b=b):
                if b > 0:
                    self.swap(b - 1).wait()
                    self.acc[...] = self.acc[...] + self.dp_recv[b - 1]
                if b < self.bits:
                    self.swap(b).start()
        for way in range(2):
            place = k if way == 0 else n - 1 - k

            @pl.when(i == self.bits + 1 + place)
            def _(way=way, place=place):
                self.line_send[way] = self.acc[...]

                @pl.when(place > 0)
                def _():
                    got = self.line_recv.at[way]
                    pltpu.make_async_copy(got, got, self.line_recv_sem.at[way]).wait()
                    self.line_send[way] = self.acc[...] + self.line_recv[way]

                @pl.when(place < n - 1)
                def _():
                    self.onward(way).start()

        @pl.when(i == self.bits + 1 + n)
        def _():
            self.acc[...] = self.line_send[0] + self.line_send[1] - self.acc[...]
            part = self.out_ref.shape[1]
            self.dp_recv[0, :, :part] = self.acc[:, pl.ds(pl.multiple_of(self.me * part, part), part)]
            self.last().start()

    def drain(self):
        @pl.when(self.k < self.n - 1)
        def _():
            self.onward(0).wait_send()

        @pl.when(self.k > 0)
        def _():
            self.onward(1).wait_send()

        self.last().wait()


def sums_kernel(n, dp, chunks, steps, ticks, groups, n_x, n_y, n_out, *refs):
    refs = list(refs)
    take = lambda count: [refs.pop(0) for _ in range(count)]
    x_ref, stats_ref, gh2_ref, gains, w_ref = take(5)
    xs, ys = take(n_x), take(n_y)
    full_ref, sum_ref = take(2)
    outs = take(n_out)
    own, recv, *line_sems = take(8)
    bits = dp.bit_length() - 1
    xbuf, ybuf, tiles = take(3)
    recvs = take(bits)
    rest = take(7)
    small_bufs, small_sems = take(4), take(5)
    k, me = lax.axis_index(AX), lax.axis_index(DP)
    line = LineSum(n, chunks, full_ref, own, recv, *line_sems)
    halving = HalvingSum(dp, groups, xs, ys, outs, xbuf, ybuf, tiles, recvs, *rest)
    small = SmallSum(n, bits, halving.partner, sum_ref, *small_bufs, small_sems)
    w, w_sem = take(2)
    streams = [Stream(ref, *take(2), True) for ref in (x_ref, stats_ref, xs[-1], gh2_ref)]
    terms = Terms(n, own, small_bufs[0], w, gains, streams)
    small_first = chunks

    w_copy = pltpu.make_async_copy(w_ref, w, w_sem.at[0])
    w_copy.start()
    terms.start(jnp.int32(0))
    halving.prologue()
    greet([(k > 0, {AX: k - 1}), (k < n - 1, {AX: k + 1})] + [(me >= 0, {DP: halving.partner(b)}) for b in range(bits)])

    small_bufs[0][...] = jnp.zeros_like(small_bufs[0])
    w_copy.wait()
    for piece in terms.pieces(jnp.int32(0)):
        piece()

    def small_step(c):
        @pl.when(c >= small_first)
        def _():
            small.step(2 * (c - small_first))
            small.step(2 * (c - small_first) + 1)

    def body(i, _):
        lines, strips = [], []
        for e in range(steps):
            c = steps * i + e
            lines += line.pieces(c)
            lines.append(functools.partial(small_step, c))
        for place in range(ticks):
            strips += halving.pieces(ticks * i + place, place, ticks)
        strips = blend(strips, terms.pieces(i + 1))
        for piece in blend(lines, strips):
            piece()
        return 0

    lax.fori_loop(0, max(-(-max(chunks + 2 * (n - 1), small_first + (bits + n + 3) // 2) // steps), -(-(halving.total + halving.lags[-1]) // ticks)), body, 0)
    line.drain()
    halving.drain(ticks)
    small.drain()


def back_sums(tokens, stats, grad_h2, gains, w_qkv, xs, ys, groups, chunks=16, slots=5, steps=2, ticks=3):
    n, dp = lax.axis_size(AX), lax.axis_size(DP)
    bits = dp.bit_length() - 1
    total, width = tokens.shape
    rows, cols = total // chunks, width // n
    w = width // dp
    block = steps * rows
    two = lambda cols, kind=jnp.bfloat16: [pltpu.VMEM((2, block, cols), kind), pltpu.SemaphoreType.DMA((2,))]
    dma = pltpu.SemaphoreType.DMA
    out_shapes = [None] * len(groups)
    for g in groups:
        size = xs[g["x"]].shape[1]
        out_shapes[g["out"]] = jax.ShapeDtypeStruct((w, size) if g["turned"] else (size, w), jnp.float32)
    anywhere = pl.BlockSpec(memory_space=pl.ANY)
    vmem = pltpu.VMEM
    low = jnp.bfloat16
    return pl.pallas_call(
        functools.partial(sums_kernel, n, dp, chunks, steps, ticks, groups, len(xs), len(ys), len(out_shapes)),
        out_shape=[jax.ShapeDtypeStruct(tokens.shape, low), jax.ShapeDtypeStruct((8, w), jnp.float32)] + out_shapes,
        in_specs=[anywhere] * 3 + [pl.BlockSpec(memory_space=vmem)] + [anywhere] * (1 + len(xs) + len(ys)),
        out_specs=[anywhere] * (2 + len(out_shapes)),
        scratch_shapes=[
            vmem((chunks, n, rows, cols), low), vmem((chunks, n + 1, rows, cols), low),
            dma((chunks, n)), dma((chunks, n + 1)), dma((chunks, n)), dma((chunks, n)), dma((chunks, n)), dma((chunks,)),
            vmem((2, total, STRIP), low), vmem((2, total, width), low), vmem((slots, *(2,) * bits, STRIP, w), low),
            *[vmem((slots, *(2,) * (bits - 1 - level), STRIP, w), low) for level in range(bits)],
            vmem((2, STRIP, w), jnp.float32), vmem((2, w, STRIP), jnp.float32),
            dma((2,)), dma((2,)), dma((bits, slots)), dma((bits, slots)), dma((2,)),
            vmem((8, width), jnp.float32), vmem((bits, 8, width), jnp.float32), vmem((2, 8, width), jnp.float32), vmem((2, 8, width), jnp.float32),
            dma((bits,)), dma((bits,)), dma((2,)), dma((2,)), dma((1,)),
            vmem(w_qkv.shape, low), dma((1,)), *two(width), *two(2, jnp.float32), *two(w_qkv.shape[1]), *two(width),
        ],
        compiler_params=pltpu.CompilerParams(collective_id=0, has_side_effects=True, vmem_limit_bytes=62 * 2**20),
        name="back_sums",
    )(tokens, stats, grad_h2, gains, w_qkv, *xs, *ys)


class LineGather:
    def __init__(self, n, chunks, rows, near_left, near_right, up_ref, right_sem, left_sem, recv_sem, hop):
        self.hop = hop
        self.n, self.chunks, self.rows, self.cols = n, chunks, rows, near_left.shape[1]
        self.near, self.up_ref, self.send_sem, self.recv_sem = (near_left, near_right), up_ref, (right_sem, left_sem), recv_sem
        self.k = lax.axis_index(AX)

    def span(self, c):
        return pl.ds(pl.multiple_of(c * self.rows, self.rows), self.rows)

    def block(self, c, j):
        return self.up_ref.at[self.span(c), pl.ds(j * self.cols, self.cols)]

    def copy(self, c, j, right, near):
        src = self.near[0 if right else 1].at[self.span(c), :] if near else self.block(c, j)
        return pltpu.make_async_remote_copy(
            src, self.block(c, j), self.send_sem[0 if right else 1].at[c, j], self.recv_sem.at[c, j],
            device_id={AX: self.k + 1 if right else self.k - 1}, device_id_type=MESH)

    def arrived(self, c, j):
        block = self.block(c, j)
        pltpu.make_async_copy(block, block, self.recv_sem.at[c, j]).wait()

    def pieces(self, i):
        return [functools.partial(self.pass_on, i, p) for p in range(self.n)]

    def pass_on(self, i, p):
        n, k = self.n, self.k
        for right in (True, False):
            j = p if right else n - 1 - p
            dist = (k - j) if right else (j - k)
            onward = (k < n - 1) if right else (k > 0)
            far = i - self.hop * (dist - 1)

            @pl.when((dist == 1) & onward & within(i, self.chunks))
            def _(j=j, right=right):
                self.copy(i, j, right, True).start()

            @pl.when((dist > 1) & within(far, self.chunks))
            def _(j=j, right=right, c=far, onward=onward):
                self.arrived(c, j)

                @pl.when(onward)
                def _():
                    self.copy(c, j, right, False).start()

    def drain(self):
        def one(c, _):
            for j in range(self.n):
                @pl.when((self.k > j) & (self.k < self.n - 1))
                def _(j=j):
                    self.copy(c, j, True, False).wait_send()

                @pl.when((self.k < j) & (self.k > 0))
                def _(j=j):
                    self.copy(c, j, False, False).wait_send()
            return 0

        lax.fori_loop(0, self.chunks, one, 0)


def gelu_and_slope(x):
    share = 0.5 * (1.0 + lax.erf(x * (0.5**0.5)))
    return x * share, share + x * (jnp.exp(-0.5 * x * x) * (2.0 * jnp.pi) ** -0.5)


def feed_kernel(
    n, chunks, tile, hop,
    h2_ref, att_ref, fc1_ref, fc2_ref, dense_ref, up_own_ref, left_ref, right_ref, x_ref,
    up_ref, hidden_ref, grad_pre_ref, grad_h2_ref, grad_att_ref, out_ref,
    own, recv, x_own, rs_send, rs_recv, out_sem, fc1, fc2, dense, h2_buf, att_buf, up_buf, hid_buf, gp_buf, gh_buf, ga_buf, slope,
    weight_sem, near_sem, h2_sem, att_sem, up_sem, hid_sem, gp_sem, gh_sem, ga_sem, *line_sems,
):
    k = lax.axis_index(AX)
    low = jnp.bfloat16
    rows = h2_buf.shape[1]
    blocks = h2_ref.shape[0] // rows
    per_block = rows // own.shape[2]
    lag = -(-(2 + hop * (n - 2)) // 2)
    cols = own.shape[3]
    rate = 3

    gather = LineGather(n, chunks, own.shape[2], left_ref, right_ref, up_ref, *line_sems, hop)
    scatter = LineScatter(n, own, recv, x_own, out_ref, rs_send, rs_recv, out_sem, hop)

    def gather_step(i):
        for piece in gather.pieces(i):
            piece()

    h2_in, att_in = Stream(h2_ref, h2_buf, h2_sem, True), Stream(att_ref, att_buf, att_sem, True)
    hid_out, gp_out = Stream(hidden_ref, hid_buf, hid_sem, False), Stream(grad_pre_ref, gp_buf, gp_sem, False)
    gh_out, ga_out = Stream(grad_h2_ref, gh_buf, gh_sem, False), Stream(grad_att_ref, ga_buf, ga_sem, False)

    h2_in.copy(jnp.int32(0)).start()
    att_in.copy(jnp.int32(0)).start()
    weights = [pltpu.make_async_copy(a, b, weight_sem.at[w]) for w, (a, b) in enumerate(((fc1_ref, fc1), (dense_ref, dense), (fc2_ref, fc2), (x_ref.at[:, pl.ds(pl.multiple_of(k * own.shape[3], own.shape[3]), own.shape[3])], x_own)))]
    for copy in weights:
        copy.start()

    def up_pieces(q):
        at, two = pl.ds(pl.multiple_of(q * rows, rows), rows), lax.rem(q, 2)
        for j in range(n):
            span = pl.ds(j * cols, cols)
            dst = up_buf.at[two, :, span]
            for cond, src in ((k == j, up_own_ref), (k - 1 == j, left_ref), (k + 1 == j, right_ref)):
                yield cond, True, pltpu.make_async_copy(src.at[at, :], dst, up_sem.at[two, j]), pltpu.make_async_copy(dst, up_ref.at[at, span], near_sem.at[two, j])
            far = (k - j > 1) | (j - k > 1)
            yield far, False, pltpu.make_async_copy(up_ref.at[at, span], dst, up_sem.at[two, j]), None

    def up_start(q):
        for cond, _, load, _ in up_pieces(q):
            @pl.when(cond)
            def _(load=load):
                load.start()

    def up_wait(q):
        for cond, near, load, put in up_pieces(q):
            @pl.when(cond)
            def _(near=near, load=load, put=put):
                load.wait()
                if near:
                    put.start()

    def up_put_wait(q):
        for cond, near, _, put in up_pieces(q):
            if near:
                @pl.when(cond)
                def _(put=put):
                    put.wait()

    greet([(k > 0, {AX: k - 1}), (k < n - 1, {AX: k + 1})])

    def forward(p):
        @pl.when(p + 1 < blocks)
        def _():
            h2_in.copy(p + 1).start()
            att_in.copy(p + 1).start()

        @pl.when(p == 0)
        def _():
            weights[0].wait()

        @pl.when(p >= 2)
        def _():
            hid_out.copy(p - 2).wait()

        h2_in.copy(p).wait()
        att_in.copy(p).wait()
        two = lax.rem(p, 2)
        keep = lax.rem(p, lag + 1)
        h2 = h2_buf[two]
        for t in range(0, fc1.shape[1], tile):
            hid, bend = gelu_and_slope(jnp.dot(h2, fc1[:, t : t + tile], preferred_element_type=jnp.float32))
            hid_buf[two, :, t : t + tile] = hid.astype(low)
            slope[keep, :, t : t + tile] = bend.astype(low)
        hid_out.copy(p).start()

        @pl.when(p == 0)
        def _():
            for copy in weights[1:]:
                copy.wait()

        att, hid = att_buf[two], hid_buf[two]
        for j in range(n):
            part = jnp.dot(hid, fc2[:, j * cols : (j + 1) * cols], preferred_element_type=jnp.float32)
            part = (part + jnp.dot(att, dense[:, j * cols : (j + 1) * cols], preferred_element_type=jnp.float32)).astype(low)
            for b in range(per_block):
                own[per_block * p + b, j] = part[b * own.shape[2] : (b + 1) * own.shape[2]]

    def backward(q):
        @pl.when(q >= 2)
        def _():
            for stream in (gp_out, gh_out, ga_out):
                stream.copy(q - 2).wait()

        up_wait(q)
        two = lax.rem(q, 2)
        keep = lax.rem(q, lag + 1)
        up = up_buf[two]
        ga_buf[two] = lax.dot_general(up, dense[...], NT, preferred_element_type=jnp.float32).astype(low)
        ga_out.copy(q).start()
        for t in range(0, fc2.shape[0], tile):
            grad = lax.dot_general(up, fc2[t : t + tile, :], NT, preferred_element_type=jnp.float32)
            gp_buf[two, :, t : t + tile] = (grad * slope[keep, :, t : t + tile].astype(jnp.float32)).astype(low)
        gp_out.copy(q).start()
        grad_pre = gp_buf[two]
        for t in range(0, fc1.shape[0], tile):
            gh_buf[two, :, t : t + tile] = lax.dot_general(grad_pre, fc1[t : t + tile, :], NT, preferred_element_type=jnp.float32).astype(low)
        gh_out.copy(q).start()

    def body(p, _):
        @pl.when(p < blocks)
        def _():
            forward(p)

        gather_step(per_block * p)
        scatter.step(lax.div(rate * p, 2))

        @pl.when(within(p - lag, blocks))
        def _():
            backward(p - lag)

        for b in range(1, per_block):
            gather_step(per_block * p + b)

        @pl.when(lax.div(rate * (p + 1), 2) - lax.div(rate * p, 2) > 1)
        def _():
            scatter.step(lax.div(rate * p, 2) + 1)

        @pl.when(within(p + 1 - lag, blocks))
        def _():
            @pl.when(p + 1 - lag >= 2)
            def _():
                up_put_wait(p - 1 - lag)

            up_start(p + 1 - lag)

        return 0

    lax.fori_loop(0, max(blocks + lag, -(-(chunks + hop * (n - 2)) // per_block), -(-2 * (scatter.chunks + hop * (n - 1)) // rate)), body, 0)
    for last in range(max(blocks - 2, 0), blocks):
        for stream in (hid_out, gp_out, gh_out, ga_out):
            stream.copy(jnp.int32(last)).wait()
        up_put_wait(jnp.int32(last))
    gather.drain()
    scatter.drain()


def feed_forward(h2, attended, fc1, fc2, dense, upstream, left, right, tokens, rows=256, chunks=16, tile=512, hop=2):
    n = lax.axis_size(AX)
    total, width = h2.shape
    hidden, heads_width, cols = fc1.shape[1], attended.shape[1], width // n
    low, dma, vmem = jnp.bfloat16, pltpu.SemaphoreType.DMA, pltpu.VMEM
    piece = total // chunks
    lag = -(-(2 + hop * (n - 2)) // 2)
    tile = min(tile, hidden)
    anywhere = pl.BlockSpec(memory_space=pl.ANY)
    shape = lambda cols: jax.ShapeDtypeStruct((total, cols), low)
    two = lambda cols: vmem((2, rows, cols), low)
    return pl.pallas_call(
        functools.partial(feed_kernel, n, chunks, tile, hop),
        out_shape=[shape(width), shape(hidden), shape(hidden), shape(width), shape(heads_width), shape(cols)],
        in_specs=[anywhere] * 9,
        out_specs=[anywhere] * 6,
        scratch_shapes=[
            *scatter_scratch(n, chunks, piece, cols),
            vmem(fc1.shape, low), vmem(fc2.shape, low), vmem(dense.shape, low),
            two(width), two(heads_width), two(width), two(hidden), two(hidden), two(width), two(heads_width), vmem((lag + 1, rows, hidden), low),
            dma((4,)), dma((2, n)), dma((2,)), dma((2,)), dma((2, n)), dma((2,)), dma((2,)), dma((2,)), dma((2,)),
            dma((chunks, n)), dma((chunks, n)), dma((chunks, n)),
        ],
        compiler_params=pltpu.CompilerParams(collective_id=1, has_side_effects=True, vmem_limit_bytes=VMEM_CAP),
        name="feed_forward",
    )(h2, attended, fc1, fc2, dense, upstream, left, right, tokens)


def attend_back_kernel(block, n, heads, qkv_ref, g_ref, o_ref, dcol_ref, drow_ref, lse_ref, rot_ref, out_ref, dk, dv):
    i = pl.program_id(1)
    scale = HEAD_DIM ** (-0.5)
    part = lambda h, c: slice((3 * h + c) * HEAD_DIM, (3 * h + c + 1) * HEAD_DIM)
    cols = lambda h: slice(h * HEAD_DIM, (h + 1) * HEAD_DIM)

    @pl.when(i == 0)
    def _():
        dk[...] = jnp.zeros_like(dk)
        dv[...] = jnp.zeros_like(dv)

    here = pl.ds(pl.multiple_of(i * block, block), block)
    docs_q = drow_ref[...]
    ones = jnp.ones((8, HEAD_DIM), jnp.float32)
    queries = [qkv_ref[here, part(h, 0)] * jnp.bfloat16(scale) for h in range(heads)]
    grads = [g_ref[:, cols(h)] for h in range(heads)]
    deltas = [
        lax.dot_general(ones, grads[h].astype(jnp.float32) * o_ref[:, cols(h)].astype(jnp.float32), NT,
                        precision=lax.Precision.HIGHEST, preferred_element_type=jnp.float32)[:1]
        for h in range(heads)
    ]
    later = lax.broadcasted_iota(jnp.int32, (block, block), 1) >= lax.broadcasted_iota(jnp.int32, (block, block), 0)

    def body(j, carry, corner=False):
        rows = pl.ds(pl.multiple_of(j * block, block), block)
        allowed = docs_q == dcol_ref[rows, :]
        if corner:
            allowed = allowed & later
        new = []
        for h in range(heads):
            q, g = queries[h], grads[h]
            k = qkv_ref[rows, part(h, 1)]
            s = lax.dot_general(k, q, NT, preferred_element_type=jnp.float32)
            p = jnp.exp(jnp.where(allowed, s - lse_ref[h], -1e30))
            dp = lax.dot_general(qkv_ref[rows, part(h, 2)], g, NT, preferred_element_type=jnp.float32)
            ds = (p * (dp - deltas[h])).astype(jnp.bfloat16)
            dv[rows, cols(h)] += jnp.dot(p.astype(jnp.bfloat16), g, preferred_element_type=jnp.float32)
            dk[rows, cols(h)] += jnp.dot(ds, q, preferred_element_type=jnp.float32)
            new.append(carry[h] + lax.dot_general(ds, k, TN, preferred_element_type=jnp.float32))
        return tuple(new)

    dq = body(i, lax.fori_loop(0, i, body, (jnp.zeros((block, HEAD_DIM), jnp.float32),) * heads), True)

    def put(rows, first, val):
        rot = rot_tiles(rot_ref[:, rows])
        out_ref[rows, first : first + LANES] = rotate_back_tile(val[:, :LANES], *rot).astype(jnp.bfloat16)
        out_ref[rows, first + LANES : first + HEAD_DIM] = val[:, LANES:].astype(jnp.bfloat16)

    for h in range(heads):
        put(here, 3 * h * HEAD_DIM, dq[h] * scale)

    @pl.when(i == n - 1)
    def _():
        for h in range(heads):
            for b in range(n):
                rows = slice(b * block, (b + 1) * block)
                put(rows, (3 * h + 1) * HEAD_DIM, dk[rows, cols(h)])
                out_ref[rows, part(h, 2)] = dv[rows, cols(h)].astype(jnp.bfloat16)


def attend_back(qkv, grad_att, attended, docs, lse, rot, block=512):
    total, cols = qkv.shape
    heads = cols // (3 * HEAD_DIM)
    seqs = total // SEQ_LEN
    n = SEQ_LEN // block
    whole = pl.BlockSpec((SEQ_LEN, cols), lambda s, i: (s, 0))
    mine = pl.BlockSpec((block, heads * HEAD_DIM), lambda s, i: (s * n + i, 0))
    table = pl.BlockSpec((ROT_DIM, SEQ_LEN), lambda s, i: (0, s))
    return pl.pallas_call(
        functools.partial(attend_back_kernel, block, n, heads),
        grid=(seqs, n),
        in_specs=[
            whole, mine, mine,
            pl.BlockSpec((SEQ_LEN, 1), lambda s, i: (s, 0)),
            pl.BlockSpec((1, block), lambda s, i: (0, s * n + i)),
            pl.BlockSpec((heads, 1, block), lambda s, i: (0, 0, s * n + i)),
            table,
        ],
        out_specs=whole,
        out_shape=jax.ShapeDtypeStruct((total, cols), jnp.bfloat16),
        scratch_shapes=[pltpu.VMEM((SEQ_LEN, heads * HEAD_DIM), jnp.float32)] * 2,
        compiler_params=pltpu.CompilerParams(vmem_limit_bytes=VMEM_CAP),
        cost_estimate=pl.CostEstimate(flops=5 * total * SEQ_LEN * heads * HEAD_DIM, bytes_accessed=8 * total * cols, transcendentals=total * SEQ_LEN),
        name="attend_back",
    )(qkv, grad_att, attended, docs[:, None], docs[None, :], lse, rot)


def on_device(tokens, segments, positions, ln1_gain, ln1_bias, ln2_gain, ln2_bias, qkv_weight, dense_weight, fc1_weight, fc2_weight, upstream):
    n = lax.axis_size(AX)
    left = lax.ppermute(upstream, AX, [(i, i + 1) for i in range(n - 1)])
    right = lax.ppermute(upstream, AX, [(i + 1, i) for i in range(n - 1)])
    rot = rot_tables(positions)
    h_one, h_two, qkv, stats = project(tokens, ln1_gain, ln1_bias, ln2_gain, ln2_bias, rot, qkv_weight)
    attended, lse = attend(qkv, segments, 1024)
    up, hidden, grad_pre, grad_h_two, grad_att, output = feed_forward(
        h_two, attended, fc1_weight, fc2_weight, dense_weight, upstream, left, right, tokens)
    grad_qkv = attend_back(qkv, grad_att, attended, segments, lse, rot)
    groups = [
        dict(x=0, y=0, count=grad_pre.shape[1] // STRIP, turned=True, out=2),
        dict(x=1, y=1, count=hidden.shape[1] // STRIP, turned=False, out=3),
        dict(x=2, y=1, count=attended.shape[1] // STRIP, turned=False, out=1),
        dict(x=3, y=2, count=grad_qkv.shape[1] // STRIP, turned=True, out=0),
    ]
    s, norm_grads, qkv_grad, dense_grad, fc1_grad, fc2_grad = back_sums(
        tokens, stats, grad_h_two, jnp.stack([ln1_gain, ln2_gain]), qkv_weight, [grad_pre, hidden, attended, grad_qkv], [h_two, up, h_one], groups)
    input_grad = finish(tokens, stats, s, up)
    return (
        output, input_grad, qkv_grad, dense_grad, fc1_grad, fc2_grad,
        norm_grads[0], norm_grads[1], norm_grads[2], norm_grads[3],
    )


def solution(mesh):
    in_specs = (
        P("dp", None),
        P("dp"),
        P("dp"),
        P(),
        P(),
        P(),
        P(),
        P(None, "tensor"),
        P("tensor", None),
        P(None, "tensor"),
        P("tensor", None),
        P("dp", "tensor"),
    )
    out_specs = (
        P("dp", "tensor"),
        P("dp", None),
        P("dp", "tensor"),
        P("tensor", "dp"),
        P("dp", "tensor"),
        P("tensor", "dp"),
        P("dp"),
        P("dp"),
        P("dp"),
        P("dp"),
    )
    return jax.shard_map(
        on_device, mesh=mesh, in_specs=in_specs, out_specs=out_specs, check_vma=False
    )
```

profile of v0, /device:TPU:0, one launch (start us, length us, event | category | flops | bytes accessed | tf_op | source)
XLA Modules:
  0.0 510.4 jit_solution(7515818177811026099)
XLA Ops:
  0.6 5.1 collective-permute-start
  5.7 1.3 collective-permute-start.1
  7.0 0.7 convert_element_type.11
  7.7 1.0 multiply_cosine_fusion
  8.7 2.0 copy.22.dcol_ref
  10.8 1.3 pad_maximum_fusion.1.refs_3_
  12.1 0.8 pad_maximum_fusion.rot_ref
  12.9 23.4 %norm_project.1 = (bf16[2048,2048]{1,0:T(8,128)(2,1)}, bf16[2048,2048]{1,0:T(8,128)(2,1)}, bf16[2048,1536]{1,0:T(8,128)(2,1)}, f32[2048,2]{1,0:T(8,128)}) custom-call(bf16[2048,2048]{1,0:T(8,128)(2,1)} %x_ref.5, f32[1,2048]{1,0:T(1,128)} %bitcast.14, f32[1,2048]{1,0:T(1,128)} %bitcast.21, f32[1,2048]{1,0:T(1,128)} %bitcast.16, f32[1,2048]{1,0:T(1,128)} %bitcast.22, ...), custom_call_target="tpu_custom_call" | custom-call | flops 12884901888 | bytes 37748736 | tf_op jit(solution)/shard_map/norm_project/pallas_call | solution.py:75
  36.3 16.7 %attend.1 = (bf16[2048,512]{1,0:T(8,128)(2,1)}, f32[2,1,2048]{2,1,0:T(1,128)}) custom-call(bf16[2048,1536]{1,0:T(8,128)(2,1)} %get-tuple-element.29.qkv_ref, s32[1,2048]{1,0:T(1,128)} %bitcast.11, s32[2048,1]{1,0:T(8,128)} %copy.22.dcol_ref), custom_call_target="tpu_custom_call" | custom-call | flops 4294967296 | bytes 12582912 | tf_op jit(solution)/shard_map/attend/pallas_call | solution.py:134
  53.0 0.0 collective-permute-done.left_ref
  53.1 0.0 copy-start.3
  53.1 1.9 collective-permute-done.1.right_ref
  55.0 0.0 copy-done.3
  55.0 164.3 %feed_forward.1 = (bf16[2048,2048]{1,0:T(8,128)(2,1)}, bf16[2048,2048]{1,0:T(8,128)(2,1)}, bf16[2048,2048]{1,0:T(8,128)(2,1)}, bf16[2048,2048]{1,0:T(8,128)(2,1)...) custom-call(bf16[2048,2048]{1,0:T(8,128)(2,1)} %get-tuple-element.28.h2_ref.refs_9_, ...), custom_call_target="tpu_custom_call" | custom-call | tf_op jit(solution)/shard_map/feed_forward/pallas_call | solution.py:1033
  219.3 32.6 %attend_back.1.refs_8_ = bf16[2048,1536]{1,0:T(8,128)(2,1)} custom-call(bf16[2048,1536]{1,0:T(8,128)(2,1)} %get-tuple-element.29.qkv_ref, bf16[2048,512]{1,0:T(8,128)(2,1)} %get-tuple-element.36.g_ref, bf16[2048,512]{1,0:T(8,128)(2,1)} %get-tuple-element.30.att_ref.o_ref.refs_7_, s32[2048,1]{1,0:T(8,128)} %copy.22.dcol_ref, s32[1,2048]{1,0:T(1,128)} %bitcast.12, ...), custom_call_target="tpu_custom_call" | custom-call | flops 10737418240 | bytes 25165824 | tf_op jit(solution)/shard_map/attend_back/pallas_call | solution.py:1118
  251.9 234.5 %back_sums.1 = (bf16[2048,2048]{1,0:T(8,128)(2,1)}, f32[8,256]{1,0:T(8,128)}, f32[256,1536]{1,0:T(8,128)}, f32[512,256]{1,0:T(8,128)}, f32[256,2048]{1,0:T(8,128)}, /*index=5*/f32[2048,256]{1,0:T(8,128)}) custom-call(bf16[2048,2048]{1,0:T(8,128)(2,1)} %x_ref.5, f32[2048,2]{1,0:T(8,128)} %get-tuple-element.32.refs_1_.stats_ref, ...), custom_call_target="tpu_custom_call" | custom-call | tf_op jit(solution)/shard_map/back_sums/pallas_call | solution.py:773
  486.4 0.0 copy-start.6
  486.4 0.0 copy-start
  486.4 0.0 copy-start.4
  486.4 17.3 %finish.1 = f32[2048,2048]{1,0:T(8,128)} custom-call(bf16[2048,2048]{1,0:T(8,128)(2,1)} %x_ref.5, f32[2048,2]{1,0:T(8,128)} %get-tuple-element.32.refs_1_.stats_ref, bf16[2048,2048]{1,0:T(8,128)(2,1)} %get-tuple-element.40.s_ref, bf16[2048,2048]{1,0:T(8,128)(2,1)} %get-tuple-element.38.refs_10_.up_ref), custom_call_target="tpu_custom_call" | custom-call | flops 41943040 | bytes 41943040 | tf_op jit(solution)/shard_map/finish/pallas_call | solution.py:164
  503.7 0.0 copy-start.5
  503.7 0.0 copy-start.2
  503.7 0.0 copy-done.6
  503.7 0.6 fusion
  504.3 0.0 copy-done
  504.3 0.0 copy-start.1
  504.3 1.3 copy.29
  505.6 0.0 copy-done.4
  505.6 1.1 copy.30
  506.8 0.0 copy-done.5
  506.8 0.8 copy.31
  507.6 0.0 copy-done.2
  507.6 1.3 copy.32
  508.9 0.0 copy-done.1
  508.9 1.3 copy.33
  (1 shorter events, 0.0 us)
Async XLA Ops:
  0.6 52.4 %collective-permute-start = (bf16[2048,512]{1,0:T(8,128)(2,1)}, bf16[2048,512]{1,0:T(8,128)(2,1)S(1)}, u32[]{:S(2)}, u32[]{:S(2)}) collective-permute-start(bf16[2048,512]{1,0:T(8,128)(2,1)} %up_own_ref.1), channel_id=1, source_target_pairs={{0,1},{1,2},{2,3},{4,5},{5,6},{6,7},{8,9},{9,10},{10,11},{12,13},{... | collective-permute-start | bytes 6291464 | tf_op jit(solution)/shard_map/ppermute | solution.py:1139
  5.7 49.3 %collective-permute-start.1 = (bf16[2048,512]{1,0:T(8,128)(2,1)}, bf16[2048,512]{1,0:T(8,128)(2,1)}, u32[]{:S(2)}, u32[]{:S(2)}) collective-permute-start(bf16[2048,512]{1,0:T(8,128)(2,1)} %up_own_ref.1), channel_id=1, source_target_pairs={{1,0},{2,1},{3,2},{5,4},{6,5},{7,6},{9,8},{10,9},{11,10},{13,12},{... | collective-permute-start | bytes 6291464 | tf_op jit(solution)/shard_map/ppermute | solution.py:1140
  53.1 2.0 copy-start.3
  486.4 17.3 %copy-start.6 = (f32[8,256]{1,0:T(8,128)S(1)}, f32[8,256]{1,0:T(8,128)}, u32[]{:S(2)}) copy-start(f32[8,256]{1,0:T(8,128)} %get-tuple-element.45) | copy-start | bytes 24580
  486.4 17.9 %copy-start = (bf16[2048,512]{1,0:T(8,128)(2,1)S(1)}, bf16[2048,512]{1,0:T(8,128)(2,1)}, u32[]{:S(2)}) copy-start(bf16[2048,512]{1,0:T(8,128)(2,1)} %get-tuple-element.62) | copy-start | bytes 6291460
  486.4 19.2 %copy-start.4 = (f32[256,1536]{1,0:T(8,128)S(1)}, f32[256,1536]{1,0:T(8,128)}, u32[]{:S(2)}) copy-start(f32[256,1536]{1,0:T(8,128)} %get-tuple-element.64) | copy-start | bytes 4718596
  503.7 3.1 copy-start.5
  503.7 3.9 copy-start.2
  504.3 4.6 copy-start.1
where the time goes:
time: 520 us; the launch traced here: 510 us
  Pallas kernels  489 us (94%)
  local copies, waits for them, and re-layouts  8.54 us (2%)
  starting transfers between devices  6.36 us (1%)
    pallas_call x1, Pallas kernels, back_sums(): pl.pallas_call(functools.partial(sums_kernel, n, dp, chunks, steps, ticks...  235 us
    pallas_call x1, Pallas kernels, feed_forward(): pl.pallas_call(functools.partial(feed_kernel, n, chunks, tile, hop), out_...  164 us
    pallas_call x1, Pallas kernels, attend_back(): pl.pallas_call(functools.partial(attend_back_kernel, block, n, heads), gr...  32.6 us
    pallas_call x1, Pallas kernels, project(): pl.pallas_call(pre_kernel, grid=(total // rows,), in_specs=[row_blk(width...  23.4 us
    pallas_call x1, Pallas kernels, finish(): pl.pallas_call(finish_kernel, grid=(total // min(rows, total),), in_specs...  17.3 us
    pallas_call x1, Pallas kernels, attend(): pl.pallas_call(functools.partial(attend_kernel, block, heads), grid=(seqs...  16.7 us
  transfers between devices with their start and end apart: 2, of which 1 were waited for; matrix products, arithmetic and copies ran while one was open for 1% of the time, Pallas kernels for 8%

commit v1 on v0

--- a/solution.py
+++ b/solution.py
@@ -862,7 +862,7 @@
     h2_ref, att_ref, fc1_ref, fc2_ref, dense_ref, up_own_ref, left_ref, right_ref, x_ref,
     up_ref, hidden_ref, grad_pre_ref, grad_h2_ref, grad_att_ref, out_ref,
     own, recv, x_own, rs_send, rs_recv, out_sem, fc1, fc2, dense, h2_buf, att_buf, up_buf, hid_buf, gp_buf, gh_buf, ga_buf, slope,
-    weight_sem, near_sem, h2_sem, att_sem, up_sem, hid_sem, gp_sem, gh_sem, ga_sem, *line_sems,
+    first_sem, weight_sem, near_sem, h2_sem, att_sem, up_sem, hid_sem, gp_sem, gh_sem, ga_sem, *line_sems,
 ):
     k = lax.axis_index(AX)
     low = jnp.bfloat16
@@ -886,7 +886,9 @@
 
     h2_in.copy(jnp.int32(0)).start()
     att_in.copy(jnp.int32(0)).start()
-    weights = [pltpu.make_async_copy(a, b, weight_sem.at[w]) for w, (a, b) in enumerate(((fc1_ref, fc1), (dense_ref, dense), (fc2_ref, fc2), (x_ref.at[:, pl.ds(pl.multiple_of(k * own.shape[3], own.shape[3]), own.shape[3])], x_own)))]
+    strips = [pl.ds(t, tile) for t in range(0, fc1.shape[1], tile)]
+    first = [pltpu.make_async_copy(fc1_ref.at[:, at], fc1.at[:, at], first_sem.at[w]) for w, at in enumerate(strips)]
+    weights = first + [pltpu.make_async_copy(a, b, weight_sem.at[w]) for w, (a, b) in enumerate(((dense_ref, dense), (fc2_ref, fc2), (x_ref.at[:, pl.ds(pl.multiple_of(k * own.shape[3], own.shape[3]), own.shape[3])], x_own)))]
     for copy in weights:
         copy.start()
 
@@ -929,10 +931,6 @@
             h2_in.copy(p + 1).start()
             att_in.copy(p + 1).start()
 
-        @pl.when(p == 0)
-        def _():
-            weights[0].wait()
-
         @pl.when(p >= 2)
         def _():
             hid_out.copy(p - 2).wait()
@@ -943,6 +941,10 @@
         keep = lax.rem(p, lag + 1)
         h2 = h2_buf[two]
         for t in range(0, fc1.shape[1], tile):
+            @pl.when(p == 0)
+            def _(t=t):
+                first[t // tile].wait()
+
             hid, bend = gelu_and_slope(jnp.dot(h2, fc1[:, t : t + tile], preferred_element_type=jnp.float32))
             hid_buf[two, :, t : t + tile] = hid.astype(low)
             slope[keep, :, t : t + tile] = bend.astype(low)
@@ -950,7 +952,7 @@
 
         @pl.when(p == 0)
         def _():
-            for copy in weights[1:]:
+            for copy in weights[len(first):]:
                 copy.wait()
 
         att, hid = att_buf[two], hid_buf[two]
@@ -1039,7 +1041,7 @@
             *scatter_scratch(n, chunks, piece, cols),
             vmem(fc1.shape, low), vmem(fc2.shape, low), vmem(dense.shape, low),
             two(width), two(heads_width), two(width), two(hidden), two(hidden), two(width), two(heads_width), vmem((lag + 1, rows, hidden), low),
-            dma((4,)), dma((2, n)), dma((2,)), dma((2,)), dma((2, n)), dma((2,)), dma((2,)), dma((2,)), dma((2,)),
+            dma((hidden // tile,)), dma((3,)), dma((2, n)), dma((2,)), dma((2,)), dma((2, n)), dma((2,)), dma((2,)), dma((2,)), dma((2,)),
             dma((chunks, n)), dma((chunks, n)), dma((chunks, n)),
         ],
         compiler_params=pltpu.CompilerParams(collective_id=1, has_side_effects=True, vmem_limit_bytes=VMEM_CAP),

time: 520 us -> 521 us (level)
  no operation moved by 1% of the time
where the time goes in v1:
time: 521 us; the launch traced here: 511 us
  Pallas kernels  489 us (94%)
  local copies, waits for them, and re-layouts  8.54 us (2%)
  starting transfers between devices  6.36 us (1%)
    pallas_call x1, Pallas kernels, back_sums(): pl.pallas_call(functools.partial(sums_kernel, n, dp, chunks, steps, ticks...  235 us
    pallas_call x1, Pallas kernels, feed_forward(): pl.pallas_call(functools.partial(feed_kernel, n, chunks, tile, hop), out_...  164 us
    pallas_call x1, Pallas kernels, attend_back(): pl.pallas_call(functools.partial(attend_back_kernel, block, n, heads), gr...  32.6 us
    pallas_call x1, Pallas kernels, project(): pl.pallas_call(pre_kernel, grid=(total // rows,), in_specs=[row_blk(width...  23.4 us
    pallas_call x1, Pallas kernels, finish(): pl.pallas_call(finish_kernel, grid=(total // min(rows, total),), in_specs...  17.3 us
    pallas_call x1, Pallas kernels, attend(): pl.pallas_call(functools.partial(attend_kernel, block, heads), grid=(seqs...  16.7 us
  transfers between devices with their start and end apart: 2, of which 1 were waited for; matrix products, arithmetic and copies ran while one was open for 1% of the time, Pallas kernels for 8%

profile of v1, /device:TPU:0, one launch (start us, length us, event | category | flops | bytes accessed | tf_op | source)
XLA Modules:
  0.0 510.6 jit_solution(4610881747228459846)
XLA Ops:
  0.6 5.1 collective-permute-start
  5.7 1.3 collective-permute-start.1
  7.0 0.7 convert_element_type.11
  7.7 1.0 multiply_cosine_fusion
  8.7 2.0 copy.22.dcol_ref
  10.8 1.3 pad_maximum_fusion.1.refs_3_
  12.1 0.8 pad_maximum_fusion.rot_ref
  12.9 23.4 %norm_project.1 = (bf16[2048,2048]{1,0:T(8,128)(2,1)}, bf16[2048,2048]{1,0:T(8,128)(2,1)}, bf16[2048,1536]{1,0:T(8,128)(2,1)}, f32[2048,2]{1,0:T(8,128)}) custom-call(bf16[2048,2048]{1,0:T(8,128)(2,1)} %x_ref.5, f32[1,2048]{1,0:T(1,128)} %bitcast.14, f32[1,2048]{1,0:T(1,128)} %bitcast.21, f32[1,2048]{1,0:T(1,128)} %bitcast.16, f32[1,2048]{1,0:T(1,128)} %bitcast.22, ...), custom_call_target="tpu_custom_call" | custom-call | flops 12884901888 | bytes 37748736 | tf_op jit(solution)/shard_map/norm_project/pallas_call | solution.py:75
  36.3 16.7 %attend.1 = (bf16[2048,512]{1,0:T(8,128)(2,1)}, f32[2,1,2048]{2,1,0:T(1,128)}) custom-call(bf16[2048,1536]{1,0:T(8,128)(2,1)} %get-tuple-element.29.qkv_ref, s32[1,2048]{1,0:T(1,128)} %bitcast.11, s32[2048,1]{1,0:T(8,128)} %copy.22.dcol_ref), custom_call_target="tpu_custom_call" | custom-call | flops 4294967296 | bytes 12582912 | tf_op jit(solution)/shard_map/attend/pallas_call | solution.py:134
  53.0 0.0 collective-permute-done.left_ref
  53.1 0.0 copy-start.3
  53.1 1.9 collective-permute-done.1.right_ref
  55.0 0.0 copy-done.3
  55.0 164.4 %feed_forward.1 = (bf16[2048,2048]{1,0:T(8,128)(2,1)}, bf16[2048,2048]{1,0:T(8,128)(2,1)}, bf16[2048,2048]{1,0:T(8,128)(2,1)}, bf16[2048,2048]{1,0:T(8,128)(2,1)...) custom-call(bf16[2048,2048]{1,0:T(8,128)(2,1)} %get-tuple-element.28.h2_ref.refs_9_, ...), custom_call_target="tpu_custom_call" | custom-call | tf_op jit(solution)/shard_map/feed_forward/pallas_call | solution.py:1035
  219.4 32.6 %attend_back.1.refs_8_ = bf16[2048,1536]{1,0:T(8,128)(2,1)} custom-call(bf16[2048,1536]{1,0:T(8,128)(2,1)} %get-tuple-element.29.qkv_ref, bf16[2048,512]{1,0:T(8,128)(2,1)} %get-tuple-element.36.g_ref, bf16[2048,512]{1,0:T(8,128)(2,1)} %get-tuple-element.30.att_ref.o_ref.refs_7_, s32[2048,1]{1,0:T(8,128)} %copy.22.dcol_ref, s32[1,2048]{1,0:T(1,128)} %bitcast.12, ...), custom_call_target="tpu_custom_call" | custom-call | flops 10737418240 | bytes 25165824 | tf_op jit(solution)/shard_map/attend_back/pallas_call | solution.py:1120
  252.0 234.5 %back_sums.1 = (bf16[2048,2048]{1,0:T(8,128)(2,1)}, f32[8,256]{1,0:T(8,128)}, f32[256,1536]{1,0:T(8,128)}, f32[512,256]{1,0:T(8,128)}, f32[256,2048]{1,0:T(8,128)}, /*index=5*/f32[2048,256]{1,0:T(8,128)}) custom-call(bf16[2048,2048]{1,0:T(8,128)(2,1)} %x_ref.5, f32[2048,2]{1,0:T(8,128)} %get-tuple-element.32.refs_1_.stats_ref, ...), custom_call_target="tpu_custom_call" | custom-call | tf_op jit(solution)/shard_map/back_sums/pallas_call | solution.py:773
  486.5 0.0 copy-start.6
  486.5 0.0 copy-start
  486.6 0.0 copy-start.4
  486.6 17.3 %finish.1 = f32[2048,2048]{1,0:T(8,128)} custom-call(bf16[2048,2048]{1,0:T(8,128)(2,1)} %x_ref.5, f32[2048,2]{1,0:T(8,128)} %get-tuple-element.32.refs_1_.stats_ref, bf16[2048,2048]{1,0:T(8,128)(2,1)} %get-tuple-element.40.s_ref, bf16[2048,2048]{1,0:T(8,128)(2,1)} %get-tuple-element.38.refs_10_.up_ref), custom_call_target="tpu_custom_call" | custom-call | flops 41943040 | bytes 41943040 | tf_op jit(solution)/shard_map/finish/pallas_call | solution.py:164
  503.8 0.0 copy-start.5
  503.8 0.0 copy-start.2
  503.8 0.0 copy-done.6
  503.8 0.6 fusion
  504.4 0.0 copy-done
  504.4 0.0 copy-start.1
  504.4 1.3 copy.29
  505.7 0.0 copy-done.4
  505.7 1.1 copy.30
  506.9 0.0 copy-done.5
  506.9 0.8 copy.31
  507.7 0.0 copy-done.2
  507.7 1.3 copy.32
  509.0 0.0 copy-done.1
  509.0 1.3 copy.33
  (1 shorter events, 0.0 us)
Async XLA Ops:
  0.6 52.4 %collective-permute-start = (bf16[2048,512]{1,0:T(8,128)(2,1)}, bf16[2048,512]{1,0:T(8,128)(2,1)S(1)}, u32[]{:S(2)}, u32[]{:S(2)}) collective-permute-start(bf16[2048,512]{1,0:T(8,128)(2,1)} %up_own_ref.1), channel_id=1, source_target_pairs={{0,1},{1,2},{2,3},{4,5},{5,6},{6,7},{8,9},{9,10},{10,11},{12,13},{... | collective-permute-start | bytes 6291464 | tf_op jit(solution)/shard_map/ppermute | solution.py:1141
  5.7 49.3 %collective-permute-start.1 = (bf16[2048,512]{1,0:T(8,128)(2,1)}, bf16[2048,512]{1,0:T(8,128)(2,1)}, u32[]{:S(2)}, u32[]{:S(2)}) collective-permute-start(bf16[2048,512]{1,0:T(8,128)(2,1)} %up_own_ref.1), channel_id=1, source_target_pairs={{1,0},{2,1},{3,2},{5,4},{6,5},{7,6},{9,8},{10,9},{11,10},{13,12},{... | collective-permute-start | bytes 6291464 | tf_op jit(solution)/shard_map/ppermute | solution.py:1142
  53.1 2.0 copy-start.3
  486.5 17.3 %copy-start.6 = (f32[8,256]{1,0:T(8,128)S(1)}, f32[8,256]{1,0:T(8,128)}, u32[]{:S(2)}) copy-start(f32[8,256]{1,0:T(8,128)} %get-tuple-element.45) | copy-start | bytes 24580
  486.5 17.9 %copy-start = (bf16[2048,512]{1,0:T(8,128)(2,1)S(1)}, bf16[2048,512]{1,0:T(8,128)(2,1)}, u32[]{:S(2)}) copy-start(bf16[2048,512]{1,0:T(8,128)(2,1)} %get-tuple-element.62) | copy-start | bytes 6291460
  486.6 19.2 %copy-start.4 = (f32[256,1536]{1,0:T(8,128)S(1)}, f32[256,1536]{1,0:T(8,128)}, u32[]{:S(2)}) copy-start(f32[256,1536]{1,0:T(8,128)} %get-tuple-element.64) | copy-start | bytes 4718596
  503.8 3.1 copy-start.5
  503.8 3.9 copy-start.2
  504.4 4.6 copy-start.1
